TPU v7x, 32 devices: a whole 2x2x4 slice. The times are simulated.
32 devices in a mesh: groups: 2 (over y), patch: 8 (over z, x), heads: 2 (over core).
Axes of the slice: x: 2, y: 2, z: 4, core: 2. Of those that a mesh axis runs over, the one named last changes fastest.
Arguments:
- hidden_in: bfloat16 [512, 1280], P(('groups', 'patch'), 'heads'), parts along dimension 0, may hold values from -150 to 150
- gn_gain: float32 [1280], P('heads'), may hold values from 0.25 to 1.75
- gn_bias: float32 [1280], P('heads'), may hold values from -3 to 3
- w_in: bfloat16 [1280, 1280], P(None, 'heads'), may hold values from -0.15625 to 0.15625
- b_in: float32 [1280], P('heads'), may hold values from -3 to 3
- ln_gain: float32 [1280], replicated, may hold values from 0.25 to 1.75
- ln_bias: float32 [1280], replicated, may hold values from -3 to 3
- w_qkv: bfloat16 [3, 1280, 1280], P(None, None, 'heads'), may hold values from -0.15625 to 0.15625
- stale_kv: bfloat16 [2, 512, 1280], P(None, ('groups', 'patch'), 'heads'), parts along dimension 1, may hold values from -64 to 64
- w_out: bfloat16 [1280, 1280], P('heads'), may hold values from -0.15625 to 0.15625
- b_out: float32 [1280], P('heads'), may hold values from -3 to 3
Outputs:
- hidden_out: float32 [512, 1280], P(('groups', 'patch'), 'heads'), parts along dimension 0
There are 2 independent parts, one for each index of `groups`. A program takes and returns all parts, laid end to end along the dimension named above; an argument that names none is the same for every part. Nothing has to cross between parts.
All inputs are finite; a program needn't handle non-finite values.
Results may differ from a plain program's by a relative error of at most 0.035.
Values may be sent and summed in bfloat16 or wider, within the bound.
A program may use at most 128 MiB of HBM per device.

v0:
```python
import jax
import jax.numpy as jnp
from jax import lax
from jax.sharding import PartitionSpec as P

C = 1280
HD = 64
GROUPS = 32


NEG_FILL = -1e30


def attend_block(queries, key_rows, val_rows, keep_mask):
    scores = jnp.einsum(
        "whd,thd->wht", queries, key_rows, preferred_element_type=jnp.float32
    ) * HD ** (-0.5)
    if keep_mask is not None:
        scores = jnp.where(keep_mask, scores, NEG_FILL)
    row_max = jnp.max(scores, axis=-1)
    weights = jnp.exp(scores - row_max[..., None])
    if keep_mask is not None:
        weights = jnp.where(keep_mask, weights, 0.0)
    weight_sum = jnp.sum(weights, axis=-1)
    out_sum = jnp.einsum(
        "wht,thd->whd", weights.astype(jnp.bfloat16), val_rows, preferred_element_type=jnp.float32
    )
    return (out_sum, row_max, weight_sum)


def merge_parts(first, second):
    out_a, max_a, sum_a = first
    out_b, max_b, sum_b = second
    both_max = jnp.maximum(max_a, max_b)
    fac_a = jnp.exp(max_a - both_max)
    fac_b = jnp.exp(max_b - both_max)
    merged_out = out_a * fac_a[..., None] + out_b * fac_b[..., None]
    return (merged_out, both_max, sum_a * fac_a + sum_b * fac_b)


def body(hidden_in, gn_gain, gn_bias, w_in, b_in, ln_gain, ln_bias, w_qkv, stale_kv, w_out, b_out):
    tok_rows, chan_half = hidden_in.shape
    full_width = ln_gain.shape[0]
    group_size = C // GROUPS
    patch_count = lax.axis_size("patch")
    cell_count = float(tok_rows * patch_count * group_size)
    values = hidden_in.astype(jnp.float32).reshape(tok_rows, chan_half // group_size, group_size)
    grp_total, grp_square = lax.psum(
        (jnp.sum(values, axis=(0, 2)), jnp.sum(values * values, axis=(0, 2))), "patch"
    )
    grp_mean = grp_total / cell_count
    grp_var = grp_square / cell_count - grp_mean * grp_mean
    centered = values - grp_mean[None, :, None]
    normed = (centered * lax.rsqrt(grp_var + 1e-06)[None, :, None]).reshape(
        tok_rows, chan_half
    ) * gn_gain + gn_bias
    normed = normed.astype(jnp.bfloat16)
    all_normed = lax.all_gather(normed, "heads", axis=1, tiled=True)
    projected = jnp.dot(all_normed, w_in, preferred_element_type=jnp.float32)
    stream = (projected + b_in).astype(jnp.bfloat16)
    stream_float = stream.astype(jnp.float32)
    tok_mean = lax.psum(jnp.sum(stream_float, axis=1), "heads") / full_width
    tok_centered = stream_float - tok_mean[:, None]
    tok_var = lax.psum(jnp.sum(tok_centered * tok_centered, axis=1), "heads") / full_width
    first_chan = lax.axis_index("heads") * chan_half
    gain_half = lax.dynamic_slice_in_dim(ln_gain, first_chan, chan_half)
    bias_half = lax.dynamic_slice_in_dim(ln_bias, first_chan, chan_half)
    norm_half = (tok_centered * lax.rsqrt(tok_var + 1e-05)[:, None] * gain_half + bias_half).astype(
        jnp.bfloat16
    )
    layer_normed = lax.all_gather(norm_half, "heads", axis=1, tiled=True)
    projections = jnp.einsum(
        "tc,icd->itd", layer_normed, w_qkv, preferred_element_type=jnp.float32
    ).astype(jnp.bfloat16)
    heads_dev = projections.shape[2] // HD
    queries = projections[0].reshape(tok_rows, heads_dev, HD)
    fresh_keys = projections[1].reshape(tok_rows, heads_dev, HD)
    fresh_vals = projections[2].reshape(tok_rows, heads_dev, HD)
    my_strip = lax.axis_index("patch")
    near_part = attend_block(queries, fresh_keys, fresh_vals, None)
    start_state = (
        jnp.zeros((tok_rows, heads_dev, HD), jnp.float32),
        jnp.full((tok_rows, heads_dev), NEG_FILL, jnp.float32),
        jnp.zeros((tok_rows, heads_dev), jnp.float32),
    )
    segment = lax.all_gather(stale_kv, "patch", axis=1, tiled=True)
    seg_len = segment.shape[1]
    key_rows = segment[0].reshape(seg_len, heads_dev, HD)
    val_rows = segment[1].reshape(seg_len, heads_dev, HD)
    positions = jnp.arange(seg_len, dtype=jnp.int32)
    keep_mask = (positions // tok_rows != my_strip)[None, None, :]
    far_part = merge_parts(start_state, attend_block(queries, key_rows, val_rows, keep_mask))
    out_sum, row_max, weight_sum = merge_parts(far_part, near_part)
    attended = (
        (out_sum / weight_sum[..., None]).astype(jnp.bfloat16).reshape(tok_rows, heads_dev * HD)
    )
    head_terms = jnp.dot(attended, w_out, preferred_element_type=jnp.float32)
    own_terms = lax.psum_scatter(head_terms, "heads", scatter_dimension=1, tiled=True)
    return stream.astype(jnp.float32) + own_terms + b_out


def solution(mesh):
    placed = (
        P(("groups", "patch"), "heads"),
        P("heads"),
        P("heads"),
        P(None, "heads"),
        P("heads"),
        P(),
        P(),
        P(None, None, "heads"),
        P(None, ("groups", "patch"), "heads"),
        P("heads", None),
        P("heads"),
    )
    return jax.shard_map(
        body, mesh=mesh, in_specs=placed, out_specs=P(("groups", "patch"), "heads"), check_vma=False
    )
```

profile of v0, /device:TPU:11, one launch (start us, length us, event | category | flops | bytes accessed | tf_op | source)
XLA Modules:
  0.0 94.3 jit_solution(6764394125459905914)
XLA Ops:
  6.6 0.9 convert_reduce_fusion
  7.5 0.1 reduce_sum.69
  7.6 0.1 reduce_sum.72
  7.7 0.1 reduce_sum.70
  7.8 0.1 reduce_sum.73
  7.9 11.6 %all-reduce = (f32[16]{0:T(128)S(1)}, f32[16]{0:T(128)S(1)}) all-reduce(f32[16]{0:T(128)S(1)} %reduce_sum.73, f32[16]{0:T(128)S(1)} %reduce_sum.70), channel_id=1, replica_groups=mesh['groups'=2,'patch'=8,'heads'=2] {'patch'}, use_global_device_ids=true, to_apply=%region_5.0 | all-reduce | flops 32 | bytes 256 | tf_op jit(solution)/shard_map/psum | solution.py:48
  19.6 0.1 mul.119
  19.7 0.1 sub.87
  19.8 0.8 fusion.24
  20.7 5.8 %all_gather.9 = bf16[32,1280]{1,0:T(8,128)(2,1)S(1)} all-gather(bf16[32,640]{1,0:T(8,128)(2,1)S(1)} %fusion.24), channel_id=1, replica_groups=mesh['groups'=2,'patch'=8,'heads'=2] {'heads'}, dimensions={1}, use_global_device_ids=true | all-gather | bytes 122880 | tf_op jit(solution)/shard_map/all_gather | solution.py:58
  26.4 1.9 %fusion.44 = (f32[32]{0:T(128)S(1)}, f32[32,640]{1,0:T(8,128)S(1)}) fusion(f32[640]{0:T(1024)} %param.15, bf16[32,1280]{1,0:T(8,128)(2,1)S(1)} %all_gather.9, bf16[1280,640]{1,0:T(8,128)(2,1)} %param.14), kind=kOutput, calls=%fused_computation.67 | convolution fusion | flops 52510688 | bytes 1804928 | tf_op jit(solution)/shard_map/dot_general | solution.py:59
  28.4 2.5 %psum.30 = f32[32]{0:T(128)S(1)} all-reduce(f32[32]{0:T(128)S(1)} %get-tuple-element.21), channel_id=1, replica_groups=mesh['groups'=2,'patch'=8,'heads'=2] {'heads'}, use_global_device_ids=true, to_apply=%region_7.0 | all-reduce | flops 32 | bytes 256 | tf_op jit(solution)/shard_map/psum | solution.py:62
  30.8 0.2 multiply_reduce_fusion
  31.0 2.5 %psum.31 = f32[32]{0:T(128)S(1)} all-reduce(f32[32]{0:T(128)S(1)} %multiply_reduce_fusion), channel_id=1, replica_groups=mesh['groups'=2,'patch'=8,'heads'=2] {'heads'}, use_global_device_ids=true, to_apply=%region_9.0 | all-reduce | flops 32 | bytes 256 | tf_op jit(solution)/shard_map/psum | solution.py:64
  33.7 0.1 add_convert_fusion
  33.8 1.9 %all_gather.10 = bf16[32,1280]{1,0:T(8,128)(2,1)S(1)} all-gather(bf16[32,640]{1,0:T(8,128)(2,1)S(1)} %add_convert_fusion), channel_id=1, replica_groups=mesh['groups'=2,'patch'=8,'heads'=2] {'heads'}, dimensions={1}, use_global_device_ids=true | all-gather | bytes 122880 | tf_op jit(solution)/shard_map/all_gather | solution.py:71
  35.6 3.4 %fusion.10 = bf16[3,32,640]{2,1,0:T(8,128)(2,1)S(1)} fusion(bf16[3,1280,640]{2,1,0:T(8,128)(2,1)} %param.18, bf16[32,1280]{1,0:T(8,128)(2,1)S(1)} %all_gather.10), kind=kOutput, calls=%fused_computation.15 | convolution fusion | flops 157347840 | bytes 5120000 | tf_op jit(solution)/shard_map/tc,icd->itd/dot_general | solution.py:72
  39.0 0.1 reshape_squeeze.15
  39.2 26.3 %all_gather.11 = bf16[2,256,640]{2,1,0:T(8,128)(2,1)S(1)} all-gather(bf16[2,32,640]{2,1,0:T(8,128)(2,1)S(1)} %copy-done.1), channel_id=1, replica_groups=mesh['groups'=2,'patch'=8,'heads'=2] {'patch'}, dimensions={1}, use_global_device_ids=true | all-gather | bytes 737280 | tf_op jit(solution)/shard_map/all_gather | solution.py:86
  65.6 0.2 copy.27
  65.8 0.1 reshape_squeeze.18
  65.9 0.1 reshape_squeeze.19
  66.1 0.2 copy.29
  66.3 0.2 fusion.45
  66.4 0.3 fusion.46
  66.7 0.2 fusion.13
  67.0 0.2 fusion.7
  67.2 0.3 fusion.9
  67.6 0.1 reshape.71
  67.7 1.0 %fusion.47 = f32[32,1280]{1,0:T(8,128)} fusion(bf16[32,640]{1,0:T(8,128)(2,1)S(1)} %reshape.71, bf16[640,1280]{1,0:T(8,128)(2,1)S(1)} %copy-done), kind=kOutput, calls=%fused_computation.70 | convolution fusion | flops 52428800 | bytes 1843200 | tf_op jit(solution)/shard_map/dot_general | solution.py:97
  68.8 17.1 %reduce-scatter.2.cloned.1.call-done = f32[32,640]{1,0:T(8,128)} async-done(((f32[32,1280]{1,0:T(8,128)}), f32[32,640]{1,0:T(8,128)}) %reduce-scatter.2.cloned.1.call-update) | async-done | bytes 81936 | tf_op jit(solution)/shard_map/reduce_scatter | solution.py:98
  85.9 1.5 %add_add_fusion = f32[32,640]{1,0:T(8,128)} fusion(f32[32,640]{1,0:T(8,128)S(1)} %get-tuple-element.22, f32[32,640]{1,0:T(8,128)} %reduce-scatter.2.cloned.1.call-done, f32[640]{0:T(1024)S(1)} %copy-done.2), kind=kLoop, calls=%fused_computation.39 | loop fusion | flops 40960 | bytes 248320 | tf_op jit(solution)/shard_map/add | solution.py:99
  (25 shorter events, 0.5 us)
Async XLA Ops:
  6.5 61.2 %copy-start = (bf16[640,1280]{1,0:T(8,128)(2,1)S(1)}, bf16[640,1280]{1,0:T(8,128)(2,1)}, u32[]{:S(2)}) copy-start(bf16[640,1280]{1,0:T(8,128)(2,1)} %param.20) | copy-start | bytes 4915204
  6.5 27.0 %copy-start.3 = (f32[1280]{0:T(1024)S(1)}, f32[1280]{0:T(1024)}, u32[]{:S(2)}) copy-start(f32[1280]{0:T(1024)} %param.16) | copy-start | bytes 15364
  6.5 27.1 %copy-start.4 = (f32[1280]{0:T(1024)S(1)}, f32[1280]{0:T(1024)}, u32[]{:S(2)}) copy-start(f32[1280]{0:T(1024)} %param.17) | copy-start | bytes 15364
  6.5 79.3 %reduce-scatter.2.cloned.1.call-start = ((), (), s32[]{:S(2)}) async-start(), calls=%async_computation.1 | async-start | bytes 245760 | tf_op jit(solution)/shard_map/reduce_scatter | solution.py:98
  35.6 3.6 %copy-start.1 = (bf16[2,32,640]{2,1,0:T(8,128)(2,1)S(1)}, bf16[2,32,640]{2,1,0:T(8,128)(2,1)}, u32[]{:S(2)}) copy-start(bf16[2,32,640]{2,1,0:T(8,128)(2,1)} %param.19) | copy-start | bytes 245764
  67.2 18.7 %copy-start.2 = (f32[640]{0:T(1024)S(1)}, f32[640]{0:T(1024)}, u32[]{:S(2)}) copy-start(f32[640]{0:T(1024)} %param.21) | copy-start | bytes 7684
Sparse Core Ops, SparseCore 0:
  68.9 16.9 reduce-scatter.1
where the time goes:
time: 95.4 us; the launch traced here: 94.3 us
  blocking collectives  50.5 us (53%)
  waiting for transfers between devices  17.1 us (18%)
  between operations  13.6 us (14%)
  matrix products  7.27 us (8%)
  other arithmetic  4.08 us (4%)
  local copies, waits for them, and re-layouts  1.67 us (2%)
    all_gather x1, blocking collectives, body(): segment = lax.all_gather(stale_kv, 'patch', axis=1, tiled=True)  26.3 us
    reduce_scatter x1, waiting for transfers between devices, body(): lax.psum_scatter(head_terms, 'heads', scatter_dimension=1, tiled=True)  17.1 us
    psum x1, blocking collectives, body(): lax.psum((jnp.sum(values, axis=(0, 2)), jnp.sum(values * values, axis=(0,...  11.6 us
    all_gather x1, blocking collectives, body(): all_normed = lax.all_gather(normed, 'heads', axis=1, tiled=True)  5.77 us
    dot_general x1, matrix products, body(): jnp.einsum('tc,icd->itd', layer_normed, w_qkv, preferred_element_type=jnp...  3.36 us
    psum x1, blocking collectives, body(): tok_mean = lax.psum(jnp.sum(stream_float, axis=1), 'heads') / full_width  2.48 us
    psum x1, blocking collectives, body(): lax.psum(jnp.sum(tok_centered * tok_centered, axis=1), 'heads') / full_width  2.47 us
    dot_general x1, matrix products, body(): projected = jnp.dot(all_normed, w_in, preferred_element_type=jnp.float32)  1.93 us
  transfers between devices with their start and end apart: 1, of which 1 were waited for; matrix products, arithmetic and copies ran while one was open for 0% of the time, Pallas kernels for 0%

commit v1 on v0

v1 whole, which is shorter than its diff:
```python
import functools
import jax
import jax.numpy as jnp
from jax import lax
from jax.experimental import pallas as pl
from jax.experimental.pallas import tpu as pltpu
from jax.sharding import PartitionSpec as P

HD = 64
GROUPS = 32
LANES = 128
MESH = pl.DeviceIdType.MESH
F32 = jnp.float32
BF16 = jnp.bfloat16


def each(first, last, action):
    if last - first <= 16:
        for index in range(first, last):
            action(index)
    else:

        def step(index, carry):
            action(index)
            return carry

        lax.fori_loop(first, last, step, 0)


def dot(a, b):
    return jnp.dot(a, b, preferred_element_type=F32)


def exact_dot(a, b):
    return jnp.dot(a, b, preferred_element_type=F32, precision=lax.Precision.HIGHEST)


def kernel(
    n,
    hidden_hbm, gain_hbm, bias_hbm, w_in_hbm, b_in_hbm, ln_gain_hbm, ln_bias_hbm,
    w_qkv_hbm, stale_hbm, w_out_hbm, b_out_hbm,
    out_ref,
    hidden, gain, bias, affine, w_in, b_in, ln_gain, ln_bias, w_qkv, w_out, b_out,
    stats_src, stats, kv, stream, terms,
    local_sem, stats_send, stats_recv, kv_send, kv_recv, pair_send, pair_recv,
):
    p = lax.axis_index("patch")
    h = lax.axis_index("heads")
    rows, half = hidden.shape[1:]
    width = 2 * half
    group_size = width // GROUPS
    cells = float(rows * n * group_size)

    def row(ref):
        return ref[...].reshape(1, -1)

    def halves(ref):
        whole = row(ref)
        low, high = whole[:, :half], whole[:, half:]
        return jnp.where(h == 0, low, high), jnp.where(h == 0, high, low)

    locals_ = []

    def fetch(src, dst):
        copy = pltpu.make_async_copy(src, dst, local_sem.at[len(locals_)])
        copy.start()
        locals_.append(copy)
        return copy

    get_hidden = fetch(hidden_hbm, hidden.at[0])

    barrier = pltpu.get_barrier_semaphore()

    def peer(d, k):
        return {"patch": lax.rem(p + d, n), "heads": h if k == 0 else 1 - h}

    def greet(k):
        def action(d):
            pl.semaphore_signal(barrier, inc=1, device_id=peer(d, k), device_id_type=MESH)

        return action

    each(1, n, greet(0))
    each(0, n, greet(1))

    get_gain = fetch(gain_hbm, gain)
    get_bias = fetch(bias_hbm, bias)
    get_b_in = fetch(b_in_hbm, b_in)
    get_w_in = fetch(w_in_hbm, w_in)
    get_ln_gain = fetch(ln_gain_hbm, ln_gain)
    get_ln_bias = fetch(ln_bias_hbm, ln_bias)
    get_qkv = [fetch(w_qkv_hbm.at[i], w_qkv.at[i]) for i in range(3)]
    get_w_out = [
        fetch(
            w_out_hbm.at[:, pl.ds(pl.multiple_of((h if k == 0 else 1 - h) * half, LANES), half)],
            w_out.at[k],
        )
        for k in (1, 0)
    ]
    get_b_out = fetch(b_out_hbm, b_out)

    chan = lax.broadcasted_iota(jnp.int32, (half, LANES), 0)
    edge = lax.broadcasted_iota(jnp.int32, (half, LANES), 1) * group_size
    to_group = ((chan >= edge) & (chan < edge + group_size)).astype(F32)
    chan = lax.broadcasted_iota(jnp.int32, (LANES, half), 1)
    edge = lax.broadcasted_iota(jnp.int32, (LANES, half), 0) * group_size
    from_group = ((chan >= edge) & (chan < edge + group_size)).astype(F32)

    get_hidden.wait()
    own = hidden[0].astype(F32)
    sums = jnp.concatenate(
        [
            jnp.sum(own, axis=0, keepdims=True),
            jnp.sum(own * own, axis=0, keepdims=True),
            jnp.zeros((6, half), F32),
        ],
        axis=0,
    )
    own_stats = exact_dot(sums, to_group)
    stats_src[...] = own_stats
    stats[0, 0] = own_stats
    get_gain.wait()
    get_bias.wait()
    affine[0, 0:1] = row(gain)
    affine[0, 1:2] = row(bias)

    pl.semaphore_wait(barrier, 2 * n - 1)

    def send_stats(k):
        def action(d):
            pltpu.make_async_remote_copy(
                src_ref=stats_src, dst_ref=stats.at[k, d],
                send_sem=stats_send.at[k], recv_sem=stats_recv.at[k],
                device_id=peer(d, k), device_id_type=MESH,
            ).start()

        return action

    each(1, n, send_stats(0))
    each(0, n, send_stats(1))

    def to_partner(index, src, dst):
        copy = pltpu.make_async_remote_copy(
            src_ref=src, dst_ref=dst,
            send_sem=pair_send.at[index], recv_sem=pair_recv.at[index],
            device_id=peer(0, 1), device_id_type=MESH,
        )
        copy.start()
        return copy

    swap_hidden = to_partner(0, hidden_hbm, hidden.at[1])
    swap_affine = to_partner(1, affine.at[0], affine.at[1])

    def send_kv(d):
        pltpu.make_async_remote_copy(
            src_ref=stale_hbm, dst_ref=kv.at[:, d],
            send_sem=kv_send, recv_sem=kv_recv,
            device_id=peer(d, 0), device_id_type=MESH,
        ).start()

    each(1, n, send_kv)

    def all_of(ref, send_sem, recv_sem):
        return pltpu.make_async_remote_copy(
            src_ref=ref, dst_ref=ref, send_sem=send_sem, recv_sem=recv_sem,
            device_id=peer(0, 1), device_id_type=MESH,
        )

    all_stats = [
        all_of(stats.at[0, pl.ds(1, n - 1)], stats_send.at[0], stats_recv.at[0]),
        all_of(stats.at[1], stats_send.at[1], stats_recv.at[1]),
    ]
    all_kv = all_of(kv.at[:, pl.ds(1, n - 1)], kv_send, kv_recv)

    swap_hidden.wait_recv()
    swap_affine.wait_recv()
    get_b_in.wait()
    get_w_in.wait()
    all_stats[0].wait_recv()
    all_stats[1].wait_recv()

    per_group = []
    for k in range(2):
        total = jnp.sum(stats[k], axis=0) / cells
        mean = total[0:1]
        per_group += [mean, lax.rsqrt(total[1:2] - mean * mean + 1e-06)]
    per_group.append(jnp.zeros((4, LANES), F32))
    per_chan = exact_dot(jnp.concatenate(per_group, axis=0), from_group)

    projected = row(b_in)
    for k in range(2):
        values = hidden[k].astype(F32)
        mean, scale = per_chan[2 * k : 2 * k + 1], per_chan[2 * k + 1 : 2 * k + 2]
        normed = ((values - mean) * scale * affine[k, 0:1] + affine[k, 1:2]).astype(BF16)
        projected = projected + dot(normed, w_in[h if k == 0 else 1 - h])
    stream[0] = projected.astype(BF16)
    swap_stream = to_partner(2, stream.at[0], stream.at[1])

    get_ln_gain.wait()
    get_ln_bias.wait()
    gains, biases = halves(ln_gain), halves(ln_bias)
    for copy in get_qkv:
        copy.wait()
    own = stream[0].astype(F32)
    own_total = jnp.sum(own, axis=1, keepdims=True)
    swap_stream.wait_recv()
    other = stream[1].astype(F32)
    tok_mean = (own_total + jnp.sum(other, axis=1, keepdims=True)) / width
    own = own - tok_mean
    other = other - tok_mean
    squares = jnp.sum(own * own, axis=1, keepdims=True) + jnp.sum(
        other * other, axis=1, keepdims=True
    )
    tok_scale = lax.rsqrt(squares / width + 1e-05)
    own = (own * tok_scale * gains[0] + biases[0]).astype(BF16)
    other = (other * tok_scale * gains[1] + biases[1]).astype(BF16)

    def project(i):
        return dot(own, w_qkv[i, h]) + dot(other, w_qkv[i, 1 - h])

    queries = project(0)
    kv[0, 0] = project(1).astype(BF16)
    kv[1, 0] = project(2).astype(BF16)
    all_kv.wait_recv()

    first_head = lax.broadcasted_iota(jnp.int32, (rows, LANES), 1) < HD
    attended = []
    for first in range(0, half, LANES):
        lanes = slice(first, first + LANES)
        query = queries[:, lanes]
        both = jnp.concatenate(
            [jnp.where(first_head, query, 0.0), jnp.where(first_head, 0.0, query)], axis=0
        ).astype(BF16)
        keys = kv[0, :, :, lanes].reshape(n * rows, LANES)
        vals = kv[1, :, :, lanes].reshape(n * rows, LANES)
        scores = lax.dot_general(
            both, keys, (((1,), (1,)), ((), ())), preferred_element_type=F32
        ) * HD ** (-0.5)
        weights = jnp.exp(scores - jnp.max(scores, axis=1, keepdims=True))
        weight_sum = jnp.sum(weights, axis=1, keepdims=True)
        mixed = dot(weights.astype(BF16), vals) / weight_sum
        attended.append(jnp.where(first_head, mixed[:rows], mixed[rows:]).astype(BF16))
    attended = jnp.concatenate(attended, axis=1)

    for copy in get_w_out:
        copy.wait()
    terms[0] = dot(attended, w_out[1])
    swap_terms = to_partner(3, terms.at[0], terms.at[1])
    get_b_out.wait()
    result = stream[0].astype(F32) + row(b_out) + dot(attended, w_out[0])
    swap_terms.wait_recv()
    out_ref[...] = result + terms[1]

    for copy in (swap_hidden, swap_affine, swap_stream, swap_terms):
        copy.wait_send()
    all_stats[0].wait_send()
    all_stats[1].wait_send()
    all_kv.wait_send()


def body(n, hidden_in, gn_gain, gn_bias, w_in, b_in, ln_gain, ln_bias, w_qkv, stale_kv, w_out, b_out):
    rows, half = hidden_in.shape
    width = ln_gain.shape[0]
    return pl.pallas_call(
        functools.partial(kernel, n),
        out_shape=jax.ShapeDtypeStruct((rows, half), F32),
        in_specs=[pl.BlockSpec(memory_space=pl.ANY)] * 11,
        out_specs=pl.BlockSpec(memory_space=pltpu.VMEM),
        scratch_shapes=[
            pltpu.VMEM((2, rows, half), BF16),
            pltpu.VMEM((half,), F32),
            pltpu.VMEM((half,), F32),
            pltpu.VMEM((2, 2, half), F32),
            pltpu.VMEM((2, half, half), BF16),
            pltpu.VMEM((half,), F32),
            pltpu.VMEM((width,), F32),
            pltpu.VMEM((width,), F32),
            pltpu.VMEM((3, 2, half, half), BF16),
            pltpu.VMEM((2, half, half), BF16),
            pltpu.VMEM((half,), F32),
            pltpu.VMEM((8, LANES), F32),
            pltpu.VMEM((2, n, 8, LANES), F32),
            pltpu.VMEM((2, n, rows, half), BF16),
            pltpu.VMEM((2, rows, half), BF16),
            pltpu.VMEM((2, rows, half), F32),
            pltpu.SemaphoreType.DMA((13,)),
            pltpu.SemaphoreType.DMA((2,)),
            pltpu.SemaphoreType.DMA((2,)),
            pltpu.SemaphoreType.DMA,
            pltpu.SemaphoreType.DMA,
            pltpu.SemaphoreType.DMA((4,)),
            pltpu.SemaphoreType.DMA((4,)),
        ],
        compiler_params=pltpu.CompilerParams(
            collective_id=0, has_side_effects=True, vmem_limit_bytes=56 * 2**20
        ),
    )(
        hidden_in,
        gn_gain,
        gn_bias,
        w_in.reshape(2, half, half),
        b_in,
        ln_gain,
        ln_bias,
        w_qkv.reshape(3, 2, half, half),
        stale_kv,
        w_out,
        b_out,
    )


def solution(mesh):
    placed = (
        P(("groups", "patch"), "heads"),
        P("heads"),
        P("heads"),
        P(None, "heads"),
        P("heads"),
        P(),
        P(),
        P(None, None, "heads"),
        P(None, ("groups", "patch"), "heads"),
        P("heads", None),
        P("heads"),
    )
    return jax.shard_map(
        functools.partial(body, mesh.shape["patch"]),
        mesh=mesh,
        in_specs=placed,
        out_specs=P(("groups", "patch"), "heads"),
        check_vma=False,
    )
```

time: 95.4 us -> 25.9 us (0.27); the launches traced: 94.3 us -> 25.7 us
  blocking collectives: 50.5 us -> 0 us
  Pallas kernels: 0 us -> 24.2 us
  waiting for transfers between devices: 17.1 us -> 0 us
  between operations: 13.6 us -> 0.01 us
  matrix products: 7.27 us -> 0 us
  other arithmetic: 4.08 us -> 0 us
    all_gather x3 -> x0, blocking collectives: 34 us -> none  [the longest x1 26.3 us: body(): segment = lax.all_gather(stale_kv, 'patch', axis=1, tiled=True)]
    pallas_call x0 -> x1, Pallas kernels: none -> 24.2 us  [body(): pl.pallas_call(functools.partial(kernel, n), out_shape=jax.ShapeDtypeStru...]
    reduce_scatter x1 -> x0, waiting for transfers between devices: 17.1 us -> none  [body(): lax.psum_scatter(head_terms, 'heads', scatter_dimension=1, tiled=True)]
    psum x3 -> x0, blocking collectives: 16.6 us -> none  [the longest x1 11.6 us: body(): lax.psum((jnp.sum(values, axis=(0, 2)), jnp.sum(values * values, axis=(0,...]
    dot_general x7 -> x0, matrix products: 7.27 us -> none  [the longest x1 3.36 us: body(): jnp.einsum('tc,icd->itd', layer_normed, w_qkv, preferred_element_type=jnp...]
    reduce_sum x6 -> x0, other arithmetic: 1.59 us -> none  [the longest x2 1.04 us: body(): jnp.sum(values, axis=(0, 2))]
    add x2 -> x0, other arithmetic: 1.55 us -> none  [the longest x1 1.53 us: body(): return stream.astype(jnp.float32) + own_terms + b_out]
    unnamed x10 -> x1, local copies, waits for them, and re-layouts: 0.02 us -> 1.53 us
  transfers between devices with their start and end apart: 1 -> 0, of which waited for: 1 -> 0; matrix products, arithmetic and copies ran while one was open for 0% -> 0% of each run, Pallas kernels for 0% -> 0%
where the time goes in v1:
time: 25.9 us; the launch traced here: 25.7 us
  Pallas kernels  24.2 us (93%)
  local copies, waits for them, and re-layouts  1.53 us (6%)
    pallas_call x1, Pallas kernels, body(): pl.pallas_call(functools.partial(kernel, n), out_shape=jax.ShapeDtypeStru...  24.2 us
    unnamed x1, local copies, waits for them, and re-layouts  1.53 us

profile of v1, /device:TPU:11, one launch (start us, length us, event | category | flops | bytes accessed | tf_op | source)
XLA Modules:
  0.0 25.7 jit_solution(10331455770468844963)
XLA Ops:
  0.0 24.2 %shard_map.109 = f32[32,640]{1,0:T(8,128)} custom-call(bf16[32,640]{1,0:T(8,128)(2,1)} %hidden_hbm.1, f32[640]{0:T(1024)} %gain_hbm.1, f32[640]{0:T(1024)} %bias_hbm.1, bf16[2,640,640]{2,1,0:T(8,128)(2,1)} %bitcast.3, f32[640]{0:T(1024)} %b_in_hbm.1, f32[1280]{0:T(1024)} %ln_gain_hbm.1, f32[1280]{0:T(1024)} %ln_bias_hbm.1, bf16[3,2,640,640]{3,2,1,0:T(8,128)(2,1)} %bitcast.2, ...), custom_call_target="tpu_custom_call" | custom-call | tf_op jit(solution)/shard_map/pallas_call | solution.py:264
  24.2 1.5 %copy.13 = f32[32,640]{1,0:T(8,128)} copy(f32[32,640]{1,0:T(8,128)} %shard_map.109) | data formatting | bytes 163840
